TPU v7x, 32 devices: a whole 2x2x4 slice. The times are simulated.
32 devices in a mesh: seq: 4 (over y, x), dp: 8 (over z, core).
Axes of the slice: x: 2, y: 2, z: 4, core: 2. Of those that a mesh axis runs over, the one named last changes fastest.
Arguments:
- tokens: bfloat16 [8, 1024, 2048], P('dp', 'seq'), may hold values from -6 to 6
- doc_ids: int32 [8, 1024], P('dp', 'seq'), may hold values from 0 to 2, as said below
- ln1_gain: bfloat16 [2048], P(('seq', 'dp')), may hold values from 0.5 to 1.5
- ln1_bias: bfloat16 [2048], P(('seq', 'dp')), may hold values from -4 to 4
- ln2_gain: bfloat16 [2048], P(('seq', 'dp')), may hold values from 0.5 to 1.5
- ln2_bias: bfloat16 [2048], P(('seq', 'dp')), may hold values from -4 to 4
- qkv_weight: bfloat16 [2048, 6144], P(('seq', 'dp')), may hold values from -0.125 to 0.125
- qkv_bias: bfloat16 [6144], P(('seq', 'dp')), may hold values from -4 to 4
- out_weight: bfloat16 [2048, 2048], P(('seq', 'dp')), may hold values from -0.75 to 0.75
- up_weight: bfloat16 [2048, 8192], P(('seq', 'dp')), may hold values from -0.125 to 0.125
- up_bias: bfloat16 [8192], P(('seq', 'dp')), may hold values from -4 to 4
- down_weight: bfloat16 [8192, 2048], P(('seq', 'dp')), may hold values from -0.0625 to 0.0625
- out_bias: bfloat16 [2048], P(('seq', 'dp')), may hold values from -4 to 4
- cotangent: bfloat16 [8, 1024, 2048], P('dp', 'seq'), may hold values from -6 to 6
Outputs:
- mixed: bfloat16 [8, 1024, 2048], P('dp', 'seq')
- input_grad: float32 [8, 1024, 2048], P('dp', 'seq')
- ln1_gain_grad: float32 [2048], P(('seq', 'dp'))
- ln1_bias_grad: float32 [2048], P(('seq', 'dp'))
- ln2_gain_grad: float32 [2048], P(('seq', 'dp'))
- ln2_bias_grad: float32 [2048], P(('seq', 'dp'))
- qkv_weight_grad: float32 [2048, 6144], P(('seq', 'dp'))
- qkv_bias_grad: float32 [6144], P(('seq', 'dp'))
- out_weight_grad: float32 [2048, 2048], P(('seq', 'dp'))
- up_weight_grad: float32 [2048, 8192], P(('seq', 'dp'))
- up_bias_grad: float32 [8192], P(('seq', 'dp'))
- down_weight_grad: float32 [8192, 2048], P(('seq', 'dp'))
- out_bias_grad: float32 [2048], P(('seq', 'dp'))
Inputs may be any that keep to these rules, and one draw needn't show every extreme that they name: `doc_ids`: each row holds three documents in order: document 0 lies within the row's first 256 tokens, document 2 within its last 256, document 1 covers all tokens between.
All inputs are finite; a program needn't handle non-finite values.
Results may differ from a plain program's by a relative error of at most 0.0092.
Values may be sent and summed in bfloat16 or wider, within the bound.
A program may use at most 448 MiB of HBM per device.

v0:
```python
import functools
import math

import jax
import jax.numpy as jnp
import numpy as np
from jax import lax
from jax.experimental import pallas as pl
from jax.experimental.pallas import tpu as pltpu
from jax.sharding import PartitionSpec as P

HEADS = 8
BF = jnp.bfloat16
F32 = jnp.float32


epsilon = 1e-05


def rotary_rows(length, rot_dims):
    half = rot_dims // 2
    exponents = np.arange(half, dtype=np.float32) * np.float32(2.0 / rot_dims)
    inverse = np.power(np.float32(10000.0), -exponents).astype(np.float32)
    phase = (np.arange(length, dtype=np.float32)[:, None] * inverse[None, :]).astype(np.float64)
    tables = np.zeros((2, length, 128), np.float32)
    tables[0] = 1.0
    tables[0, :, :half] = tables[0, :, half:rot_dims] = np.cos(phase)
    tables[1, :, :half] = -np.sin(phase)
    tables[1, :, half:rot_dims] = np.sin(phase)
    return tables


def dot(left, right):
    return jnp.dot(left, right, preferred_element_type=F32)


MESH = pl.DeviceIdType.MESH


def run(when, action):
    if when is None:
        action()
    else:
        pl.when(when)(lambda: action())


class Net:
    def __init__(self, seq_n, dp_n, send_sems, recv_sems, local_sems):
        self.S, self.DP, self.Z = seq_n, dp_n, dp_n // 2
        self.s, self.d = lax.axis_index("seq"), lax.axis_index("dp")
        self.z, self.c = self.d // 2, lax.rem(self.d, 2)
        self.send_sems, self.recv_sems, self.used = send_sems, recv_sems, 0
        self.local_sems, self.local_used = local_sems, 0
        self.sent = []

    def seq_peer(self, s):
        return (s, self.d)

    def line_peer(self, z):
        return (self.s, 2 * jnp.clip(z, 0, self.Z - 1) + self.c)

    def partner(self):
        return (self.s, 2 * self.z + 1 - self.c)

    def copy(self, src, dst, device):
        self.used += 1
        return self.copy_at(self.used - 1, src, dst, device)

    def copy_at(self, i, src, dst, device):
        return pltpu.make_async_remote_copy(
            src_ref=src,
            dst_ref=dst,
            send_sem=self.send_sems.at[i],
            recv_sem=self.recv_sems.at[i],
            device_id=device,
            device_id_type=MESH,
        )

    def send(self, copy, when=None):
        self.sent.append((copy, when))
        run(when, copy.start)

    def drain(self):
        for copy, when in self.sent:
            run(when, copy.wait_send)

    def near(self, src, dst):
        self.local_used += 1
        return pltpu.make_async_copy(src, dst, self.local_sems.at[self.local_used - 1])

    def barrier(self):
        sem = pltpu.get_barrier_semaphore()
        peers = [self.seq_peer(lax.rem(self.s + k, self.S)) for k in range(1, self.S)]
        peers += [(self.s, lax.rem(self.d + k, self.DP)) for k in range(1, self.DP)]
        for device in peers:
            pl.semaphore_signal(sem, inc=1, device_id=device, device_id_type=MESH)
        pl.semaphore_wait(sem, len(peers))


class Place:
    def __init__(self, net, direct, through):
        self.direct = [net.near(src, dst) for src, dst in direct]
        self.loads = [net.near(src, buf) for src, buf, _ in through]
        self.stores = [net.near(buf, dst) for _, buf, dst in through]

    def start(self):
        for copy in self.loads + self.direct:
            copy.start()

    def finish(self):
        for load, store in zip(self.loads, self.stores):
            load.wait()
            store.start()
        for copy in self.stores + self.direct:
            copy.wait()


class Exchange:
    def __init__(self, net, src, slot, by_turn=False, own=False, settle=False):
        self.net, self.copies, self.settle = net, [], settle
        for k in range(1, net.S):
            to = lax.rem(net.s + k, net.S)
            self.copies.append(net.copy(src(to), slot(k - 1 if by_turn else net.s), net.seq_peer(to)))
        self.own = net.near(src(net.s), slot(net.s)) if own else None

    def start(self):
        for copy in self.copies:
            if self.settle:
                copy.start()
            else:
                self.net.send(copy)
        if self.own is not None:
            self.own.start()

    def wait(self):
        for copy in self.copies:
            copy.wait_recv()
            if self.settle:
                copy.wait_send()
        if self.own is not None:
            self.own.wait()


class GatherSeq:
    def __init__(self, net, src, slot):
        self.net, self.square = net, net.S == 4
        if self.square:
            s = net.s
            a, b = s + 1 - 2 * lax.rem(s, 2), lax.rem(s + 2, 4)
            self.first = [net.copy(src, slot(s, None), net.seq_peer(p)) for p in (a, b)]
            self.second = [
                net.copy(slot(a, 0), slot(a, 0), net.seq_peer(b)),
                net.copy(slot(b, 1), slot(b, 1), net.seq_peer(a)),
            ]
        else:
            self.direct = Exchange(net, lambda to: src, lambda k: slot(k, None))

    def start(self):
        if self.square:
            for copy in self.first:
                self.net.send(copy)
        else:
            self.direct.start()

    def relay(self):
        if self.square:
            for came, onward in zip(self.first, self.second):
                came.wait_recv()
                self.net.send(onward)

    def wait(self):
        if self.square:
            for copy in self.second:
                copy.wait_recv()
        else:
            self.direct.wait()


class SumSeq:
    def __init__(self, net, src, came, onward, held):
        self.net, self.src, self.came, self.onward, self.held, self.square = net, src, came, onward, held, net.S == 4
        if not self.square:
            self.direct = Exchange(net, lambda k: src.at[k], lambda k: came.at[k], by_turn=True)
            return
        s, half = net.s, src.shape[1] // 2
        a, b, across = s + 1 - 2 * lax.rem(s, 2), lax.rem(s + 2, 4), 3 - s
        self.ways = (b, a)
        part = lambda k, h: src.at[k, pl.ds(h * half, half)]
        self.first = []
        for h, near in ((0, a), (1, b)):
            for i, block in enumerate((near, across)):
                self.first.append(net.copy(part(block, h), came.at[2 * h + i], net.seq_peer(near)))
        self.second = [net.copy(held.at[h], onward.at[h], net.seq_peer(to)) for h, to in ((0, b), (1, a))]

    def start(self):
        if self.square:
            for i in (1, 3, 0, 2):
                self.net.send(self.first[i])
        else:
            self.direct.start()

    def mid(self):
        if not self.square:
            return
        b, a = self.ways
        half, width = self.held.shape[1:]
        for i in (1, 3):
            self.first[i].wait_recv()

        def body(own, other, o):
            o[...] = (own[...].astype(F32) + other[...].astype(F32)).astype(BF)

        block = (1, half, width)
        stream(
            body,
            (2,),
            [
                (self.src, block, lambda h: (jnp.where(h == 0, b, a), h, 0)),
                (self.came, block, lambda h: (2 * h + 1, 0, 0)),
            ],
            [(self.held, block, lambda h: (h, 0, 0))],
        )
        for copy in self.second:
            self.net.send(copy)

    def wait(self):
        if self.square:
            for i in (0, 2):
                self.first[i].wait_recv()
            for copy in self.second:
                copy.wait_recv()
        else:
            self.direct.wait()

    def ins(self, rows):
        if self.square:
            block = (1, rows, self.src.shape[2])
            return [(self.came, block, lambda i: (2 * i, 0, 0)), (self.onward, block, lambda i: (i, 0, 0))]
        return [(self.came, (self.net.S - 1, rows, self.src.shape[2]), lambda i: (0, i, 0))]


class Line:
    def go(self, part):
        last = self.net.Z - 1
        for t in ([1], range(2, last), [last])[part - 1]:
            self.step(t)


class GatherLine(Line):
    def __init__(self, net, slab, own=None):
        self.net = net
        z, c, last = net.z, net.c, net.Z - 1
        own = slab(net.d) if own is None else own
        self.right, self.left = [], []
        for t in range(net.Z):
            for side, hops in ((1, self.right), (-1, self.left)):
                place = slab(2 * jnp.clip(z - side * t, 0, last) + c)
                src = own if t == 0 else place
                there = z >= t if side == 1 else z <= last - t
                onward = z < last if side == 1 else z > 0
                copy = None if t == last else net.copy(src, place, net.line_peer(z + side))
                core = None if t == 0 and side == -1 else net.copy(src, place, net.partner())
                hops.append((copy, there & onward, core, None if t == 0 else there))

    def early(self):
        self.net.send(self.right[0][0], self.net.z == 0)
        self.net.send(self.left[0][0], self.net.z == self.net.Z - 1)

    def start(self):
        inside = (self.net.z > 0) & (self.net.z < self.net.Z - 1)
        self.net.send(self.right[0][0], inside)
        self.net.send(self.left[0][0], inside)
        self.net.send(self.right[0][2])

    def step(self, t):
        for hops in (self.right, self.left):
            copy, sends, core, there = hops[t]
            run(there, hops[t - 1][0].wait_recv)
            if copy is not None:
                self.net.send(copy, sends)
            self.net.send(core, there)

    def wait(self):
        for hops in (self.right, self.left):
            for _, _, core, there in hops:
                if core is not None:
                    run(there, core.wait_recv)


def add_slabs(dst, left, right):
    blocks, rows = dst.shape[0], dst.shape[1]
    per = rows // 16

    @pl.loop(0, blocks * per)
    def _(i):
        at = (i // per, pl.ds(pl.multiple_of(lax.rem(i, per) * 16, 16), 16), slice(None))
        dst[at] = (left[at].astype(F32) + right[at].astype(F32)).astype(dst.dtype)


class ReduceLine(Line):
    def __init__(self, net, part, own, mate, from_left, from_right):
        self.net, self.own, self.mate, self.bufs = net, own, mate, (from_left, from_right)
        z, c, Z = net.z, net.c, net.Z
        self.order = []
        for t in range((Z + 1) // 2):
            self.order += [Z - 1 - t] + ([t] if t != Z - 1 - t else [])
        self.swaps = {k: net.copy(part(2 * k + 1 - c), mate.at[k], net.partner()) for k in self.order}
        self.loads = {k: net.near(part(2 * k + c), own.at[k]) for k in self.order}
        self.base = net.used
        net.used += 2 * (Z - 1)
        ends = (jnp.clip(Z - 1 - z, 0, Z - 2), jnp.clip(z, 0, Z - 2))
        self.last = [net.near(buf.at[t], mate.at[i]) for i, (buf, t) in enumerate(zip(self.bufs, ends))]

    def start(self):
        for k in self.order:
            self.net.send(self.swaps[k])
            self.loads[k].start()

    def hop(self, side, t):
        net, last = self.net, self.net.Z - 1
        place, way = (last - t, 0) if side == 1 else (t, 1)
        return net.copy_at(
            self.base + way * last + t, self.own.at[place], self.bufs[way].at[t], net.line_peer(net.z + side)
        )

    def pair(self):
        net, done = self.net, set()
        last = net.Z - 1
        right, left = last, 0
        for k in self.order:
            self.loads[k].wait()
            self.swaps[k].wait_recv()
            add_slabs(self.own.at[k], self.own.at[k], self.mate.at[k])
            done.add(k)
            while right > 0 and right in done:
                net.send(self.hop(1, last - right), net.z == 0)
                right -= 1
            while left < last and left in done:
                net.send(self.hop(-1, left), net.z == last)
                left += 1

    def step(self, n):
        net = self.net
        z, last = net.z, net.Z - 1
        for side, far, way in ((1, z, 0), (-1, last - z, 1)):
            t = jnp.clip(n - far, 0, last - 1)
            here = (far >= 1) & (far <= n)
            hop = self.hop(side, t)
            run(here, hop.wait_recv)
            if n < last:
                place, held = last - t if side == 1 else t, self.mate.at[way]
                load = net.near(self.bufs[way].at[t], held)

                def add():
                    load.start()
                    load.wait()
                    add_slabs(self.own.at[place], self.own.at[place], held)

                run(here, add)
                net.send(hop, here)

    def total(self, out=None):
        z, last = self.net.z, self.net.Z - 1
        out = self.own.at[z] if out is None else out
        here = (z > 0, z < last)
        for copy, when in zip(self.last, here):
            run(when, copy.start)
        for copy, when in zip(self.last, here):
            run(when, copy.wait)
        per = out.shape[1] // 16

        def body(ways):
            @pl.loop(0, out.shape[0] * per)
            def _(i):
                at = (i // per, pl.ds(pl.multiple_of(lax.rem(i, per) * 16, 16), 16), slice(None))
                value = self.own.at[z][at].astype(F32)
                for way in ways:
                    value = value + self.mate[(way,) + at].astype(F32)
                out[at] = value.astype(out.dtype)

        run(z == 0, lambda: body((1,)))
        run(z == last, lambda: body((0,)))
        if last > 1:
            run((z > 0) & (z < last), lambda: body((0, 1)))


ANY = pl.BlockSpec(memory_space=pl.ANY)
MIB = 1024 * 1024
HD = 256
shape = jax.ShapeDtypeStruct


def nt(left, right):
    return lax.dot_general(left, right, (((1,), (1,)), ((), ())), preferred_element_type=F32)


def tn(left, right):
    return lax.dot_general(left, right, (((0,), (0,)), ((), ())), preferred_element_type=F32)


def turn(value, cosine, sine):
    half = HD // 8
    first = lax.broadcasted_iota(jnp.int32, value.shape, 1) < half
    other = jnp.where(first, pltpu.roll(value, 128 - half, 1), pltpu.roll(value, half, 1))
    return value * cosine + other * sine


def stream(body, grid, ins, outs):
    def spec(entry):
        block, index = entry[1:3]
        return pl.BlockSpec(block, index, pipeline_mode=pl.Buffered(1)) if len(entry) > 3 else pl.BlockSpec(block, index)

    pltpu.emit_pipeline(
        body, grid=grid, in_specs=[spec(e) for e in ins], out_specs=[spec(e) for e in outs]
    )(*[e[0] for e in ins], *[e[0] for e in outs])


def whole(ref):
    return (ref, ref.shape, lambda *i: (0,) * len(ref.shape), 1)


def chunks(rows, size):
    return lambda body: pl.loop(0, rows // size)(lambda i: body(pl.ds(pl.multiple_of(i * size, size), size), i))


def layer_kernel(seq_n, dp_n, dims, n_ins, n_outs, *refs):
    ins, outs = refs[:n_ins], refs[n_ins : n_ins + n_outs]
    scratch = refs[n_ins + n_outs :]
    x_own, gy_own, up_w, qkv_w, out_w, down_w, small, tables = ins
    mixed_out, input_grad, qkv_red, out_red, down_red, small_red = outs[:6]
    up_red, mixed_bufs, wide_bufs = outs[6:8], outs[8:11], outs[11:14]
    x, qkv_all, out_all, heads, gatt, wide_f, p_qkv, p_out, mixed, wide = outs[14:24]
    up_all, down_all, slope, p_up, p_down = [outs[24 + 2 * i : 26 + 2 * i] for i in range(5)]
    hops = outs[34:]
    sems, scratch = scratch[:3], scratch[3:]
    small_v, vec, up_b, qkv_b, doc_row, cols_v, sm, sm_dp, sm_sum, dk_acc, dv_acc = scratch[:11]
    out_f, down_f, tab, gy, n1, n2, hidden, att, gproj = scratch[11:20]
    scratch = scratch[20:]
    mean_at, inv_at, doc_at = [slice(k, k + 1) for k in range(3)]
    grad_up = n1
    L, D, ff, H, r, ro, rd = dims
    hd = HD
    T, CH = (HD, 512) if L <= 1024 else (HD // 2, 256)
    l, ffh, rdh, half_n = H * hd, ff // 2, rd // 2, 2
    net = Net(seq_n, dp_n, *sems)
    S, Z, s, d = net.S, net.Z, net.s, net.d
    tok = L // S
    scale = 1.0 / math.sqrt(hd)
    per = dp_n * r // T
    own_rows = pl.ds(pl.multiple_of(s * tok, tok), tok)

    def lanes(ref):
        return (ref, (ref.shape[0], T), lambda i: (0, i))

    def d_rows(ref):
        return (ref, (1, T // r, r, ref.shape[3]), lambda i: (lax.div(i, per), lax.rem(i, per), 0, 0))

    def reduce(i, part):
        return ReduceLine(net, part, scratch[2 * i], scratch[2 * i + 1], hops[2 * i], hops[2 * i + 1])

    def seq_rows(ref):
        def slot(k, h):
            size = tok if h is None else tok // 2
            return ref.at[pl.ds(pl.multiple_of(k * tok + (h or 0) * size, size), size)]

        return slot

    halves = range(half_n)
    x_g, gy_g = GatherSeq(net, x_own, seq_rows(x)), GatherSeq(net, gy_own, seq_rows(gy))
    up_cut = scratch[7]
    su = [
        Exchange(net, lambda k, h=h: up_cut.at[h, k], lambda k, h=h: up_all[h].at[k, d], own=True, settle=True)
        for h in halves
    ]
    sq = [
        Exchange(
            net,
            lambda k, j=j: qkv_w.at[:, pl.ds(pl.multiple_of((j * S + k) * l, 128), l)],
            lambda k, j=j: qkv_all.at[k, d, :, pl.ds(j * l, l)],
        )
        for j in range(3)
    ]
    o_g = GatherLine(net, lambda k: out_all.at[k], out_w)
    q_g = GatherLine(net, lambda k: qkv_all.at[:, k])
    u_g = [GatherLine(net, lambda k, h=h: up_all[h].at[:, k]) for h in halves]
    down_rows = [down_w.at[pl.ds(h * rdh, rdh)] for h in halves]
    d_g = [GatherLine(net, lambda k, h=h: down_all[h].at[k], down_rows[h]) for h in halves]
    ds = [reduce(h, lambda k, h=h: p_down[h].at[pl.ds(k, 1)]) for h in halves]
    us = [reduce(2 + h, lambda k, h=h: p_up[h].at[:, k]) for h in halves]
    qs = reduce(4, lambda k: p_qkv.at[:, k])
    os = reduce(5, lambda k: p_out.at[pl.ds(k, 1)])
    mx = SumSeq(net, mixed, *mixed_bufs)
    wx = SumSeq(net, wide, *wide_bufs)
    qx = Exchange(net, lambda k: qs.own.at[net.z, k], lambda k: qkv_red.at[k], own=True)
    ux = [Exchange(net, lambda k, h=h: us[h].own.at[net.z, k], lambda k, h=h: up_red[h].at[k], own=True) for h in halves]
    sf = Exchange(net, lambda k: small_v.at[s], lambda k: small_v.at[k])
    sm_x = Exchange(net, lambda k: sm_sum, lambda k: small_red.at[k], own=True)
    small_to = [lax.rem(d + k, dp_n) for k in range(1, dp_n)]
    small_from = [lax.rem(d + dp_n - k, dp_n) for k in range(1, dp_n)]
    sf_dp = [net.copy(small, small_v.at[s, d], (s, to)) for to in small_to]
    sm_to = [net.copy(sm, sm_dp.at[d], (s, to)) for to in small_to]
    sf_own = net.near(small, small_v.at[s, d])
    spot = lambda at, rows, base, width: n1.at[pl.ds(at, rows), pl.ds(base, width)]
    loc = Place(
        net,
        [(gy_own, gy.at[own_rows]), (tables, tab)],
        [
            (
                qkv_w.at[:, pl.ds(pl.multiple_of((j * S + s) * l, 128), l)],
                spot(tok + ro, r, j * l, l),
                qkv_all.at[s, d, :, pl.ds(j * l, l)],
            )
            for j in range(3)
        ]
        + [(x_own, spot(0, tok, 0, D), x.at[own_rows]), (out_w, spot(tok, ro, 0, D), out_all.at[d])]
        + [(down_rows[h], scratch[2 * h].at[0, 0], down_all[h].at[d]) for h in halves],
    )
    up_loads = [net.near(up_w.at[:, pl.ds(k * ff, ff)], n2.at[pl.ds(k * r, r), pl.ds(0, ff)]) for k in range(S)]
    out_copies = [net.near(out_f, out_red)] + [net.near(down_f, down_red.at[:, pl.ds(h * rdh, rdh)]) for h in halves]
    begun = []

    def out_total():
        os.total(out_f)
        out_copies[0].start()

    def down_total(h):
        for copy in begun:
            copy.wait()
        ds[h].total(down_f)
        out_copies[1 + h].start()
        begun[:] = [out_copies[1 + h]]

    def cut_up():
        for k, load in enumerate(up_loads):
            load.wait()
            rows = slice(k * r, (k + 1) * r)
            for m in range(dp_n):
                for h in halves:
                    up_cut[h, k, :, m * rdh : (m + 1) * rdh] = n2[rows, m * rd + h * rdh : m * rd + (h + 1) * rdh]

    def small_first():
        sf_own.start()
        for copy in sf_dp:
            net.send(copy)

    def small_second():
        sf_own.wait()
        for copy in sf_dp:
            copy.wait_recv()
        sf.start()

    def sums_first():
        for copy in sm_to:
            net.send(copy)

    def sums_second():
        sm_sum[...] = sm[...]
        for copy, source in zip(sm_to, small_from):
            copy.wait_recv()
            sm_sum[...] += sm_dp[source]
        sm_x.start()

    def pieces(out, row, found):
        lane = lax.broadcasted_iota(jnp.int32, (1, 128), 1) // r
        q = 128 // r
        for p in range(len(found) // q):
            value = small_v[found[p * q]]
            for k in range(1, q):
                value = jnp.where(lane == k, small_v[found[p * q + k]], value)
            out[row : row + 1, 128 * p : 128 * p + 128] = value

    def unpack():
        sf.wait()
        for j in range(5):
            pieces(vec, j, [(i // dp_n, i % dp_n, slice(j, j + 1)) for i in range(seq_n * dp_n)])
        for h in halves:
            pieces(up_b, h, [(s, m // 2, slice(8 + 2 * h + m % 2, 9 + 2 * h + m % 2)) for m in range(2 * dp_n)])
        found = []
        for j in range(3):
            for m in range(l // r):
                piece = j * (D // r) + s * (l // r) + m
                owner = lax.div(piece, 3)
                found.append((lax.div(owner, dp_n), lax.rem(owner, dp_n), pl.ds(5 + lax.rem(piece, 3), 1)))
        pieces(qkv_b, 0, found)
        for k in range(S):
            for j in range(tok // 128):
                row = small_v[k, d, 12 + j : 13 + j]
                at = k * tok + j * 128
                doc_row[0:1, at : at + 128] = row
                cols_v[at : at + 128, :] = jnp.transpose(jnp.broadcast_to(row, (128, 128)))
        sm[...] = jnp.zeros_like(sm)
        sm[4:5, :] = jnp.sum(gy[own_rows, :].astype(F32), 0, keepdims=True)

    def cols_of(base=0):
        return pl.ds(pl.multiple_of(base + pl.program_id(0) * T, T), T)

    def norm_phase():
        def body(xb):
            i = pl.program_id(0)
            at = pl.ds(pl.multiple_of(i * T, T), T)
            wide_x = xb[...].astype(F32)
            mean = jnp.mean(wide_x, -1, keepdims=True)
            center = wide_x - mean
            inv = lax.rsqrt(jnp.mean(center * center, -1, keepdims=True) + epsilon)
            cols_v[at, mean_at] = mean
            cols_v[at, inv_at] = inv
            hat = center * inv
            n1[at, :] = (hat * vec[0:1, :] + vec[1:2, :]).astype(BF)
            n2[at, :] = (hat * vec[2:3, :] + vec[3:4, :]).astype(BF)

        stream(body, (L // T,), [(x, (T, D), lambda i: (i, 0))], [])

    def up_phase(h):
        def body(w, slo):
            cols = cols_of(h * ffh)
            bias = up_b[h : h + 1, cols_of()]

            @chunks(L, CH)
            def _(at, i):
                u = dot(n2[at, :], w[...].reshape(D, T)) + bias
                phi = 0.5 + 0.5 * lax.erf(u * math.sqrt(0.5))
                hidden[at, cols] = (u * phi).astype(BF)
                slo[at, :] = (phi + u * (jnp.exp(-0.5 * u * u) * (1.0 / math.sqrt(2.0 * math.pi)))).astype(BF)

        stream(body, (ffh // T,), [(up_all[h], (S, dp_n, r, T), lambda i: (0, 0, 0, i))], [lanes(slope[h])])

    def outer_phase(left, base, n, right, out):
        def body(o):
            width = o.shape[-1]
            step = min(width, 1024)

            @chunks(width, step)
            def _(at, j):
                value = tn(left[:, cols_of(base)], right[:, at])
                o[(slice(None),) * (len(o.shape) - 1) + (at,)] = value.astype(BF).reshape(o.shape[:-1] + (step,))

        if len(out.shape) == 3:
            target = (out, (T // out.shape[1], out.shape[1], D), lambda i: (i, 0, 0))
        else:
            target = d_rows(out)
        stream(body, (n,), [], [target])

    def down_grad_phase(h):
        outer_phase(hidden, h * ffh, ffh // T, gy, p_down[h])

    def up_grad_phase(h):
        outer_phase(n2, 0, D // T, grad_up.at[:, pl.ds(h * ffh, ffh)], p_up[h])

    def out_grad_phase():
        outer_phase(att, 0, l // T, gy, p_out)

    def qkv_grad_phase():
        def body(o):
            for j in range(3):
                o[:, :, :, j * l : (j + 1) * l] = tn(n1[:, cols_of()], gproj[j]).astype(BF).reshape(o.shape[:-1] + (l,))

        for j in range(3):
            sm[6:7, j * l : (j + 1) * l] = jnp.sum(gproj[j].astype(F32), 0, keepdims=True)
        stream(body, (D // T,), [], [d_rows(p_qkv)])

    def gatt_phase():
        def body(w, o):
            @chunks(L, CH)
            def _(at, i):
                o[0, at, :] = nt(gy[at, :], w[...].reshape(hd, D)).astype(BF)

        w = (out_all, (hd // ro, ro, D), lambda i: (i, 0, 0))
        stream(body, (H,), [w], [(gatt, (1, L, hd), lambda i: (i, 0, 0))])

    def qkv_phase():
        def body(w, o):
            j = pl.program_id(0)
            bias = qkv_b[0:1, pl.ds(pl.multiple_of(j * hd, hd), hd)]

            @chunks(L, CH)
            def _(at, i):
                p = dot(n1[at, :], w[...].reshape(D, hd)) + bias
                o[0, at, 128:] = p[:, 128:].astype(BF)

                @pl.when(j < 2 * H)
                def _():
                    o[0, at, :128] = turn(p[:, :128], tab[0, at, :], tab[1, at, :]).astype(BF)

                @pl.when(j >= 2 * H)
                def _():
                    o[0, at, :128] = p[:, :128].astype(BF)

        w = (qkv_all, (S, dp_n, r, hd), lambda i: (0, 0, 0, i))
        stream(body, (3 * H,), [w], [(heads, (1, L, hd), lambda i: (i, 0, 0))])

    def att_phase():
        def body(q, k, v, ga):
            h, i = pl.program_id(0), pl.program_id(1)
            cols = pl.ds(pl.multiple_of(h * hd, hd), hd)
            low = pl.ds(pl.multiple_of(h * hd, hd), 128)
            high = pl.ds(pl.multiple_of(h * hd + 128, 128), 128)
            back = lambda t, rows: turn(t, tab[0, rows, :], -tab[1, rows, :])

            @pl.when(i == 0)
            def _():
                dk_acc[...] = jnp.zeros_like(dk_acc)
                dv_acc[...] = jnp.zeros_like(dv_acc)

            def tile(c):
                n = (c + 1) * T
                at = slice(c * T, n)
                qt, kt, vt, gt = q[0], k[0, :n], v[0, :n], ga[0]
                query = lax.broadcasted_iota(jnp.int32, (T, n), 0) + c * T
                key = lax.broadcasted_iota(jnp.int32, (T, n), 1)
                allowed = (cols_v[at, doc_at] == doc_row[0:1, :n]) & (key <= query)
                raw = jnp.where(allowed, nt(qt, kt) * scale, -1000000000.0)
                e = jnp.exp(raw - jnp.max(raw, -1, keepdims=True))
                p = e / jnp.sum(e, -1, keepdims=True)
                pb = p.astype(BF)
                att[at, cols] = dot(pb, vt).astype(BF)
                gp = nt(gt, vt)
                gs = (p * (gp - jnp.sum(gp * p, -1, keepdims=True))).astype(BF)
                gq = dot(gs, kt) * scale
                gproj[0, at, low] = back(gq[:, :128], at).astype(BF)
                gproj[0, at, high] = gq[:, 128:].astype(BF)
                dk_acc[:n, :] += tn(gs, qt)
                dv_acc[:n, :] += tn(pb, gt)

            for c in range(L // T):
                pl.when(i == c)(functools.partial(tile, c))

            @pl.when(i == L // T - 1)
            def _():
                gk = dk_acc[...] * scale
                gproj[1, :, low] = back(gk[:, :128], slice(None)).astype(BF)
                gproj[1, :, high] = gk[:, 128:].astype(BF)
                gproj[2, :, cols] = dv_acc[...].astype(BF)

        block = (1, T, hd)
        full = (1, L, hd)
        stream(
            body,
            (H, L // T),
            [
                (heads, block, lambda h, i: (h, i, 0)),
                (heads, full, lambda h, i: (H + h, 0, 0)),
                (heads, full, lambda h, i: (2 * H + h, 0, 0)),
                (gatt, block, lambda h, i: (h, i, 0)),
            ],
            [],
        )

    def norm_sums(grad, xb, at, row):
        cols = cols_of()
        hat = (xb[at, :].astype(F32) - cols_v[at, mean_at]) * cols_v[at, inv_at]
        sm[row : row + 1, cols] += jnp.sum(grad * hat, 0, keepdims=True)
        sm[row + 1 : row + 2, cols] += jnp.sum(grad, 0, keepdims=True)

    def one_phase():
        def body(w, xb, o):
            @chunks(L, CH)
            def _(at, m):
                grad = 0.0
                for j in range(3):
                    grad = grad + nt(gproj[j, at, :], w[:, :, :, j * l : (j + 1) * l].reshape(T, l))
                norm_sums(grad, xb, at, 0)
                o[at, :] = grad * vec[0:1, cols_of()]

        stream(body, (D // T,), [d_rows(qkv_all), lanes(x)], [lanes(wide_f)])

    per_ch = max(1, CH // tok)

    def two_phase():
        def body(wa, wb, xb, first, o):
            @chunks(L, per_ch * tok)
            def _(at, m):
                grad = nt(grad_up[at, :ffh], wa[...].reshape(T, ffh)) + nt(grad_up[at, ffh:ff], wb[...].reshape(T, ffh))
                norm_sums(grad, xb, at, 2)
                value = first[at, :] + grad * vec[2:3, cols_of()]
                o[pl.ds(m * per_ch, per_ch)] = value.astype(BF).reshape(per_ch, tok, T)

        stream(
            body,
            (D // T,),
            [d_rows(up_all[0]), d_rows(up_all[1]), lanes(x), lanes(wide_f)],
            [(wide, (S, tok, T), lambda i: (0, 0, i))],
        )

    def mixed_phase():
        def body(wa, wb, wo, o):
            @chunks(L, per_ch * tok)
            def _(at, m):
                value = dot(hidden[at, :ffh], wa[...].reshape(ffh, T)) + dot(hidden[at, ffh:], wb[...].reshape(ffh, T))
                value = value + dot(att[at, :], wo[...].reshape(l, T))
                o[pl.ds(m * per_ch, per_ch)] = value.astype(BF).reshape(per_ch, tok, T)

        cols = lambda ref: (ref, ref.shape[:2] + (T,), lambda i: (0, 0, i))
        ws = [cols(down_all[0]), cols(down_all[1]), cols(out_all)]
        stream(body, (D // T,), ws, [(mixed, (S, tok, T), lambda i: (0, 0, i))])

    def slope_phase(h):
        def body(w, slo):
            cols = cols_of(h * ffh)

            @chunks(L, CH)
            def _(at, m):
                gu = (nt(gy[at, :], w[...].reshape(T, D)) * slo[at, :].astype(F32)).astype(BF)
                grad_up[at, cols] = gu
                sm[5:6, cols] += jnp.sum(gu.astype(F32), 0, keepdims=True)

        w = (down_all[h], (T // rdh, rdh, D), lambda i: (i, 0, 0))
        stream(body, (ffh // T,), [w, lanes(slope[h])], [])

    ends = 2 if mx.square else 8
    part = tok // ends
    tiles = lambda ref, lead: (ref, (lead, part, D), lambda i: (0, i, 0))
    mine = lambda ref: (ref, (part, D), lambda i: (i, 0))

    def total_of(own, came):
        total = own[0].astype(F32)
        for ref in came:
            for k in range(ref.shape[0]):
                total = total + ref[k].astype(F32)
        return total

    def mixed_end():
        def body(xb, own, *rest):
            rest[-1][0] = (xb[...].astype(F32) + vec[4:5, :] + total_of(own, rest[:-1])).astype(BF)

        stream(body, (ends,), [mine(x_own), tiles(mixed.at[pl.ds(s, 1)], 1)] + mx.ins(part), [tiles(mixed_out, 1)])

    def input_end():
        def body(xb, gb, own, *rest):
            at = pl.ds(pl.multiple_of(s * tok + pl.program_id(0) * part, part), part)
            inv = cols_v[at, inv_at]
            hat = (xb[...].astype(F32) - cols_v[at, mean_at]) * inv
            total = total_of(own, rest[:-1])
            total = total - jnp.mean(total, -1, keepdims=True) - hat * jnp.mean(total * hat, -1, keepdims=True)
            rest[-1][0] = gb[...].astype(F32) + inv * total

        ins = [mine(x_own), mine(gy_own), tiles(wide.at[pl.ds(s, 1)], 1)] + wx.ins(part)
        stream(body, (ends,), ins, [tiles(input_grad, 1)])

    net.barrier()
    loc.start()
    for load in up_loads:
        load.start()
    small_first()
    o_g.early()
    o_g.start()
    for x_sq in sq:
        x_sq.start()
    cut_up()
    su[0].start()
    o_g.go(1)
    loc.finish()
    for x_sq in sq:
        x_sq.wait()
    q_g.early()
    q_g.start()
    x_g.start()
    su[0].wait()
    u_g[0].early()
    o_g.go(2)
    u_g[0].start()
    o_g.go(3)
    small_second()
    x_g.relay()
    gy_g.start()
    u_g[0].go(1)
    u_g[0].go(2)
    x_g.wait()
    unpack()
    norm_phase()
    u_g[0].go(3)
    d_g[1].early()
    q_g.go(1)
    gy_g.relay()
    su[1].start()
    u_g[0].wait()
    up_phase(0)
    d_g[0].early()
    q_g.go(2)
    gy_g.wait()
    down_grad_phase(0)
    su[1].wait()
    u_g[1].early()
    ds[0].start()
    u_g[1].start()
    o_g.wait()
    d_g[1].start()
    ds[0].pair()
    d_g[0].start()
    q_g.go(3)
    gatt_phase()
    q_g.wait()
    qkv_phase()
    att_phase()
    out_grad_phase()
    os.start()
    d_g[0].go(1)
    u_g[1].go(1)
    os.pair()
    qkv_grad_phase()
    qs.start()
    ds[0].go(1)
    qs.pair()
    d_g[0].go(2)
    one_phase()
    d_g[0].go(3)
    u_g[1].go(2)
    d_g[1].go(1)
    d_g[0].wait()
    slope_phase(0)
    qs.go(1)
    up_grad_phase(0)
    u_g[1].go(3)
    u_g[1].wait()
    d_g[1].go(2)
    os.go(1)
    us[0].start()
    up_phase(1)
    ds[0].go(2)
    d_g[1].go(3)
    us[0].pair()
    d_g[1].wait()
    mixed_phase()
    qs.go(2)
    mx.start()
    slope_phase(1)
    up_grad_phase(1)
    us[1].start()
    os.go(2)
    qs.go(3)
    qs.total()
    qx.start()
    us[0].go(1)
    us[1].pair()
    down_grad_phase(1)
    mx.mid()
    us[0].go(2)
    us[1].go(1)
    two_phase()
    sums_first()
    wx.start()
    us[0].go(3)
    us[0].total()
    ds[1].start()
    us[1].go(2)
    sums_second()
    ds[0].go(3)
    ds[1].pair()
    ds[1].go(1)
    down_total(0)
    qx.wait()
    us[1].go(3)
    mx.wait()
    mixed_end()
    us[1].total()
    ux[1].start()
    wx.mid()
    ds[1].go(2)
    ux[0].start()
    wx.wait()
    os.go(3)
    ux[1].wait()
    input_end()
    ds[1].go(3)
    out_total()
    down_total(1)
    ux[0].wait()
    sm_x.wait()
    for copy in [out_copies[0]] + begun:
        copy.wait()
    net.drain()


def layer(seq_n, dp_n, dims, args):
    L, D, ff, H, r, ro, rd = dims
    l, Z, ffh, rdh = H * HD, dp_n // 2, ff // 2, rd // 2
    tok = L // seq_n
    seq_tok, up_slab, qkv_slab = (seq_n, tok, D), (seq_n, r, ffh), (seq_n, r, 3 * l)
    outs = [((1, tok, D), BF), ((1, tok, D), F32), (qkv_slab, BF), ((1, ro, D), F32), ((1, rd, D), F32), ((seq_n, 8, D), F32)]
    outs += [(up_slab, BF)] * 2
    half = tok // 2
    if seq_n == 4:
        outs += [((4, half, D), BF), ((2, half, D), BF), ((2, half, D), BF)] * 2
    else:
        outs += [((seq_n - 1, tok, D), BF), ((16, 128), BF), ((16, 128), BF)] * 2
    outs += [((L, D), BF), ((seq_n, dp_n, r, 3 * l), BF), ((dp_n, ro, D), BF), ((3 * H, L, HD), BF), ((H, L, HD), BF)]
    outs += [((L, D), F32), ((seq_n, dp_n, r, 3 * l), BF), ((dp_n, ro, D), BF), (seq_tok, BF), (seq_tok, BF)]
    up_full, down_full = (seq_n, dp_n, r, ffh), (dp_n, rdh, D)
    for v in (up_full, down_full, (L, ffh), up_full, down_full):
        outs += [(v, BF)] * 2
    slabs = [(1, rdh, D)] * 2 + [up_slab] * 2 + [qkv_slab, (1, ro, D)]
    for slab in slabs:
        outs += [((Z - 1,) + slab, BF)] * 2
    out_shape = [shape(*o) for o in outs]
    n = 6 * (4 * Z - 3) + 6 * (3 * Z - 2) + 14 * (seq_n - 1) + 2 * max(4, seq_n - 1) + 2 * (dp_n - 1)
    vmem = [((seq_n, dp_n, 16, 128), F32), ((8, D), F32), ((8, ffh), F32), ((8, 3 * l), F32), ((8, L), F32), ((L, 128), F32)]
    vmem += [((8, D), F32), ((dp_n, 8, D), F32), ((8, D), F32), ((L, HD), F32), ((L, HD), F32)]
    vmem += [((1, ro, D), F32), ((1, rdh, D), F32), ((2, L, 128), F32)]
    vmem += [((L, D), BF), ((L, D), BF), ((L, D), BF), ((L, ff), BF), ((L, l), BF), ((3, L, l), BF)]
    for slab in slabs:
        vmem += [((Z,) + slab, BF)] * 2
    scratch = [pltpu.SemaphoreType.DMA((k,)) for k in (n, n, 40 + seq_n + 6 * (3 * Z - 2))] + [pltpu.VMEM(*v) for v in vmem]
    return pl.pallas_call(
        functools.partial(layer_kernel, seq_n, dp_n, dims, len(args), len(outs)),
        out_shape=out_shape,
        in_specs=[ANY] * len(args),
        out_specs=[ANY] * len(outs),
        scratch_shapes=scratch,
        compiler_params=pltpu.CompilerParams(collective_id=0, has_side_effects=True, vmem_limit_bytes=63 * MIB),
        name="layer",
    )(*args)[:8]


def last_kernel(dims, seq_n, dp_n, places, *refs):
    L, D, ff, H, r, ro, rd = dims
    l, ffh, rdh = H * HD, ff // 2, rd // 2
    ins, outs, acc = refs[:8], refs[8:-1], refs[-1]
    mixed, grad, qkv, out_w, down, sums, up_a, up_b = ins
    mixed_out, grad_out, up_out, qkv_out, out_out, down_out = outs[:6]
    small = outs[6:]
    mixed_out[...] = mixed[...]
    grad_out[...] = grad[...]
    out_out[...] = out_w[0]
    down_out[...] = down[0]
    for k in range(seq_n):
        for m in range(dp_n):
            for h, src in enumerate((up_a, up_b)):
                at = k * ff + m * rd + h * rdh
                up_out[:, at : at + rdh] = src[k, :, m * rdh : (m + 1) * rdh].astype(F32)
        for j in range(3):
            at = (j * seq_n + k) * l
            qkv_out[:, at : at + l] = qkv[k, :, j * l : (j + 1) * l].astype(F32)

    @pl.when(pl.program_id(0) == 0)
    def _():
        s, d = places[0], places[1]
        place = s * dp_n + d
        acc[...] = sums[0]
        for k in range(1, seq_n):
            acc[...] += sums[k]

        def piece(load, lane):
            start = pl.multiple_of(lax.div(lane, 128) * 128, 128)
            return pltpu.roll(load(pl.ds(start, 128)), lax.rem(128 - lax.rem(lane, 128), 128), 1)

        for j in range(5):
            small[j][...] = piece(lambda at, j=j: acc[j : j + 1, at], place * r)[:, :r]
        for t in range(3):
            at = place * 3 + t
            j, rest = lax.div(at, D // r), lax.rem(at, D // r)
            of, m = lax.div(rest, l // r), lax.rem(rest, l // r)
            small[5][:, t * r : (t + 1) * r] = piece(lambda at, of=of: sums[of, 6:7, at], j * l + m * r)[:, :r]
        for h in range(2):
            small[6][:, h * rdh : (h + 1) * rdh] = piece(lambda at: sums[s, 5:6, at], h * ffh + d * rdh)[:, :rdh]


def finish(seq_n, dp_n, dims, got):
    L, D, ff, H, r, ro, rd = dims
    tok = L // seq_n
    steps = 4 if r % 64 == 0 else 1
    places = jnp.stack([lax.axis_index("seq"), lax.axis_index("dp")]).astype(jnp.int32)

    def spec(v, axis):
        block = tuple(n // steps if k == axis else n for k, n in enumerate(v.shape))
        return pl.BlockSpec(block, lambda i, p: tuple(i if k == axis else 0 for k in range(v.ndim)))

    outs = [((1, tok, D), BF, 1), ((1, tok, D), F32, 1), ((r, seq_n * ff), F32, 0), ((r, 3 * D), F32, 0), ((ro, D), F32, 0), ((rd, D), F32, 0)]
    outs += [((1, r), F32, None)] * 5 + [((1, 3 * r), F32, None), ((1, rd), F32, None)]
    out_shape = [shape(*o[:2]) for o in outs]
    return pl.pallas_call(
        functools.partial(last_kernel, dims, seq_n, dp_n),
        grid_spec=pltpu.PrefetchScalarGridSpec(
            num_scalar_prefetch=1,
            grid=(steps,),
            in_specs=[spec(v, axis) for v, axis in zip(got, (1, 1, 1, 1, 1, None, 1, 1))],
            out_specs=[spec(v, o[2]) for v, o in zip(out_shape, outs)],
            scratch_shapes=[pltpu.VMEM((8, D), F32)],
        ),
        out_shape=out_shape,
        compiler_params=pltpu.CompilerParams(vmem_limit_bytes=63 * MIB),
        name="finish",
    )(places, *got)
def shards(
    tokens,
    doc_ids,
    ln1_gain,
    ln1_bias,
    ln2_gain,
    ln2_bias,
    qkv_weight,
    qkv_bias,
    out_weight,
    up_weight,
    up_bias,
    down_weight,
    out_bias,
    cotangent,
):
    seq_n = lax.axis_size("seq")
    dp_n = lax.axis_size("dp")
    seq_i = lax.axis_index("seq")
    tok_rows, width = tokens.shape[1:]
    length = tok_rows * seq_n
    head_dim = width // HEADS
    heads = HEADS // seq_n
    local = heads * head_dim
    ff = up_weight.shape[1] // seq_n
    rot_dims = head_dim // 4
    rows, per_down = qkv_weight.shape[0], down_weight.shape[0]
    vectors = (ln1_gain, ln1_bias, ln2_gain, ln2_bias, out_bias, qkv_bias, up_bias)
    total, at, flat = sum(v.shape[0] for v in vectors), 0, 0.0
    for v in vectors:
        flat = flat + jnp.pad(v.astype(F32), (at, total - at - v.shape[0]))
        at += v.shape[0]
    pieces = jnp.tile(flat.reshape(-1, rows), (1, 128 // rows))
    docs = doc_ids.astype(F32).reshape(-1, 128)
    over = 16 - pieces.shape[0]
    small = jnp.pad(pieces, ((0, over), (0, 0))) + jnp.pad(docs, ((16 - over, over - docs.shape[0]), (0, 0)))
    dims = (length, width, ff, heads, rows, out_weight.shape[0], per_down)
    tables = jnp.asarray(rotary_rows(length, rot_dims))
    x, gy = tokens[0], cotangent[0]
    got = layer(seq_n, dp_n, dims, (x, gy, up_weight, qkv_weight, out_weight, down_weight, small, tables))
    mixed, input_grad, up_grad, qkv_grad, out_grad, down_grad, *small = finish(seq_n, dp_n, dims, got)
    g1, b1, g2, b2, ob, qb, ub = [v.reshape(-1) for v in small]
    return (mixed, input_grad, g1, b1, g2, b2, qkv_grad, qb, out_grad, up_grad, ub, down_grad, ob)


def solution(mesh):
    in_specs = (
        P("dp", "seq", None),
        P("dp", "seq"),
        P(("seq", "dp")),
        P(("seq", "dp")),
        P(("seq", "dp")),
        P(("seq", "dp")),
        P(("seq", "dp"), None),
        P(("seq", "dp")),
        P(("seq", "dp"), None),
        P(("seq", "dp"), None),
        P(("seq", "dp")),
        P(("seq", "dp"), None),
        P(("seq", "dp")),
        P("dp", "seq", None),
    )
    out_specs = (
        P("dp", "seq", None),
        P("dp", "seq", None),
        P(("seq", "dp")),
        P(("seq", "dp")),
        P(("seq", "dp")),
        P(("seq", "dp")),
        P(("seq", "dp"), None),
        P(("seq", "dp")),
        P(("seq", "dp"), None),
        P(("seq", "dp"), None),
        P(("seq", "dp")),
        P(("seq", "dp"), None),
        P(("seq", "dp")),
    )
    return jax.shard_map(shards, mesh=mesh, in_specs=in_specs, out_specs=out_specs, check_vma=False)
```

profile of v0, /device:TPU:0, one launch (start us, length us, event | category | flops | bytes accessed | tf_op | source)
XLA Modules:
  0.0 358.9 jit_solution(8779998936790207302)
XLA Ops:
  0.6 0.8 convert_add_fusion
  1.5 0.1 tile.10
  1.6 0.1 tile.12
  1.6 0.7 convert_element_type.16
  2.3 0.6 pad_add_fusion.refs_6_
  2.9 347.2 %layer.1 = (bf16[1,256,2048]{2,1,0:T(8,128)(2,1)}, f32[1,256,2048]{2,1,0:T(8,128)}, bf16[4,64,1536]{2,1,0:T(8,128)(2,1)}, f32[1,64,2048]{2,1,0:T(8,128)}, f32[1,...) custom-call(bf16[256,2048]{1,0:T(8,128)(2,1)} %bitcast.12, ...), custom_call_target="tpu_custom_call" | custom-call | tf_op jit(solution)/shard_map/layer/pallas_call | solution.py:1002
  350.2 0.7 pad_add_fusion.1.places
  350.9 7.8 %finish.1 = (bf16[1,256,2048]{2,1,0:T(8,128)(2,1)}, f32[1,256,2048]{2,1,0:T(8,128)}, f32[64,8192]{1,0:T(8,128)}, f32[64,6144]{1,0:T(8,128)}, f32[64,2048]{1,0:T(...) custom-call(s32[2]{0:T(128)} %pad_add_fusion.1.places, ...), custom_call_target="tpu_custom_call" | custom-call | tf_op jit(solution)/shard_map/finish/pallas_call | solution.py:1069
  (1 shorter events, 0.0 us)
where the time goes:
time: 363 us; the launch traced here: 359 us
  Pallas kernels  355 us (98%)
    pallas_call x1, Pallas kernels, layer(): pl.pallas_call(functools.partial(layer_kernel, seq_n, dp_n, dims, len(arg...  347 us
    pallas_call x1, Pallas kernels, finish(): pl.pallas_call(functools.partial(last_kernel, dims, seq_n, dp_n), grid_sp...  7.85 us

commit v1 on v0

--- a/solution.py
+++ b/solution.py
@@ -843,127 +843,127 @@
     small_first()
     o_g.early()
     o_g.start()
-    for x_sq in sq:
-        x_sq.start()
     cut_up()
     su[0].start()
     o_g.go(1)
+    x_g.start()
+    for x_sq in sq:
+        x_sq.start()
     loc.finish()
+    su[0].wait()
+    u_g[0].early()
+    u_g[0].start()
+    o_g.go(2)
+    d_g[0].early()
+    u_g[0].go(1)
+    small_second()
+    x_g.relay()
     for x_sq in sq:
         x_sq.wait()
     q_g.early()
+    gy_g.start()
+    u_g[0].go(2)
+    u_g[0].go(3)
+    d_g[1].early()
+    u_g[0].wait()
     q_g.start()
-    x_g.start()
-    su[0].wait()
-    u_g[0].early()
-    o_g.go(2)
-    u_g[0].start()
-    o_g.go(3)
-    small_second()
-    x_g.relay()
-    gy_g.start()
-    u_g[0].go(1)
-    u_g[0].go(2)
     x_g.wait()
     unpack()
     norm_phase()
-    u_g[0].go(3)
-    d_g[1].early()
+    o_g.go(3)
     q_g.go(1)
     gy_g.relay()
+    up_phase(0)
+    q_g.go(2)
     su[1].start()
-    u_g[0].wait()
-    up_phase(0)
-    d_g[0].early()
-    q_g.go(2)
+    d_g[1].start()
     gy_g.wait()
     down_grad_phase(0)
     su[1].wait()
     u_g[1].early()
     ds[0].start()
+    o_g.wait()
+    gatt_phase()
+    q_g.go(3)
+    q_g.wait()
     u_g[1].start()
-    o_g.wait()
-    d_g[1].start()
     ds[0].pair()
+    qkv_phase()
     d_g[0].start()
-    q_g.go(3)
-    gatt_phase()
-    q_g.wait()
-    qkv_phase()
     att_phase()
     out_grad_phase()
     os.start()
+    os.pair()
     d_g[0].go(1)
     u_g[1].go(1)
-    os.pair()
     qkv_grad_phase()
     qs.start()
+    os.go(1)
+    d_g[0].go(2)
     ds[0].go(1)
     qs.pair()
-    d_g[0].go(2)
     one_phase()
     d_g[0].go(3)
     u_g[1].go(2)
     d_g[1].go(1)
     d_g[0].wait()
     slope_phase(0)
+    u_g[1].go(3)
     qs.go(1)
     up_grad_phase(0)
-    u_g[1].go(3)
+    us[0].start()
     u_g[1].wait()
     d_g[1].go(2)
-    os.go(1)
-    us[0].start()
     up_phase(1)
+    us[0].pair()
+    d_g[1].go(3)
+    d_g[1].wait()
+    slope_phase(1)
+    qs.go(2)
+    two_phase()
+    sums_first()
+    us[0].go(1)
+    wx.start()
     ds[0].go(2)
-    d_g[1].go(3)
-    us[0].pair()
-    d_g[1].wait()
-    mixed_phase()
-    qs.go(2)
-    mx.start()
-    slope_phase(1)
     up_grad_phase(1)
     us[1].start()
-    os.go(2)
+    sums_second()
     qs.go(3)
     qs.total()
     qx.start()
-    us[0].go(1)
+    us[0].go(2)
     us[1].pair()
+    mixed_phase()
+    mx.start()
+    us[1].go(1)
     down_grad_phase(1)
+    us[0].go(3)
+    os.go(2)
+    us[1].go(2)
+    ds[1].start()
+    us[0].total()
+    wx.mid()
+    os.go(3)
+    out_total()
+    ds[1].pair()
+    ux[0].start()
+    ds[1].go(1)
     mx.mid()
-    us[0].go(2)
-    us[1].go(1)
-    two_phase()
-    sums_first()
-    wx.start()
-    us[0].go(3)
-    us[0].total()
-    ds[1].start()
-    us[1].go(2)
-    sums_second()
+    us[1].go(3)
+    ds[1].go(2)
+    ux[0].wait()
+    qx.wait()
+    wx.wait()
+    us[1].total()
     ds[0].go(3)
-    ds[1].pair()
-    ds[1].go(1)
+    ux[1].start()
+    input_end()
     down_total(0)
-    qx.wait()
-    us[1].go(3)
     mx.wait()
     mixed_end()
-    us[1].total()
-    ux[1].start()
-    wx.mid()
-    ds[1].go(2)
-    ux[0].start()
-    wx.wait()
-    os.go(3)
+    ds[1].go(3)
+    down_total(1)
     ux[1].wait()
-    input_end()
-    ds[1].go(3)
-    out_total()
-    down_total(1)
-    ux[0].wait()
     sm_x.wait()
     for copy in [out_copies[0]] + begun:
         copy.wait()

time: 363 us -> 362 us (level)
  no operation moved by 1% of the time
where the time goes in v1:
time: 362 us; the launch traced here: 360 us
  Pallas kernels  357 us (99%)
    pallas_call x1, Pallas kernels, layer(): pl.pallas_call(functools.partial(layer_kernel, seq_n, dp_n, dims, len(arg...  349 us
    pallas_call x1, Pallas kernels, finish(): pl.pallas_call(functools.partial(last_kernel, dims, seq_n, dp_n), grid_sp...  7.85 us

profile of v1, /device:TPU:0, one launch (start us, length us, event | category | flops | bytes accessed | tf_op | source)
XLA Modules:
  0.0 360.4 jit_solution(9051191540682130108)
XLA Ops:
  0.6 0.8 convert_add_fusion
  1.5 0.1 tile.10
  1.6 0.1 tile.12
  1.6 0.7 convert_element_type.16
  2.3 0.6 pad_add_fusion.refs_6_
  2.9 348.8 %layer.1 = (bf16[1,256,2048]{2,1,0:T(8,128)(2,1)}, f32[1,256,2048]{2,1,0:T(8,128)}, bf16[4,64,1536]{2,1,0:T(8,128)(2,1)}, f32[1,64,2048]{2,1,0:T(8,128)}, f32[1,...) custom-call(bf16[256,2048]{1,0:T(8,128)(2,1)} %bitcast.12, ...), custom_call_target="tpu_custom_call" | custom-call | tf_op jit(solution)/shard_map/layer/pallas_call | solution.py:1002
  351.7 0.7 pad_add_fusion.1.places
  352.4 7.8 %finish.1 = (bf16[1,256,2048]{2,1,0:T(8,128)(2,1)}, f32[1,256,2048]{2,1,0:T(8,128)}, f32[64,8192]{1,0:T(8,128)}, f32[64,6144]{1,0:T(8,128)}, f32[64,2048]{1,0:T(...) custom-call(s32[2]{0:T(128)} %pad_add_fusion.1.places, ...), custom_call_target="tpu_custom_call" | custom-call | tf_op jit(solution)/shard_map/finish/pallas_call | solution.py:1069
  (1 shorter events, 0.0 us)
